TPU v7x, 512 devices: a whole 4x8x8 slice. The times are simulated.
512 devices in a mesh: sta: 128 (over y, z, core), win: 4 (over x).
Axes of the slice: x: 4, y: 8, z: 8, core: 2. Of those that a mesh axis runs over, the one named last changes fastest.
Arguments:
- spectra: bfloat16 [256, 4, 2, 2048], P('sta', 'win'), may hold values from -6 to 6
- masks: int32 [256, 4], P('sta'), may hold values 0 or 1
- pairs: int32 [16384, 2], P('sta'), may hold values from 0 to 255
- owners: int32 [16384, 1], P('sta'), may hold values from 0 to 127; in each aligned block of 128 rows (0 to 127, 128 to 255, ...) at most 2 rows name the same one
Outputs:
- stacks: float32 [32768, 512], P('sta', 'win')
Inputs may be any that keep to these rules, and one draw needn't show every extreme that they name: `owners`: within each aligned block of 128 rows no owner is named more than 2 times, a bound that some block reaches.
All inputs are finite; a program needn't handle non-finite values. No bound on the sum of `masks` on one device may be relied on, other than what follows from the above.
Results may differ from a plain program's by a relative error of at most 0.0023.
Values may be sent and summed in bfloat16 or wider, within the bound.
A program may use at most 64 MiB of HBM per device.

v0:
```python
import math

import jax
import jax.numpy as jnp
from jax import lax
from jax.sharding import PartitionSpec as P

LAGS = 512
FIRST_BIN = 360
SAMPLES = 180000


def lag_table(bins, lags):
    freq = lax.broadcasted_iota(jnp.int32, (bins, lags), 0) + FIRST_BIN
    lag = lax.broadcasted_iota(jnp.int32, (bins, lags), 1) - lags // 2
    turns = freq * lag % SAMPLES
    angle = turns.astype(jnp.float32) * (2.0 * math.pi / SAMPLES)
    scale = bins ** (-0.5)
    return jnp.concatenate([jnp.cos(angle) * scale, -jnp.sin(angle) * scale], 0)


def correlate(every, every_mask, first_ids, second_ids, live, win_dev, parts_two, bins):
    nrows = first_ids.shape[0]
    stations = every.shape[0]
    column = lax.broadcasted_iota(jnp.int32, (nrows, stations), 1)
    pick_first = ((first_ids[:, None] == column) & (live[:, None] > 0)).astype(jnp.bfloat16)
    pick_second = ((second_ids[:, None] == column) & (live[:, None] > 0)).astype(jnp.bfloat16)
    first = jnp.dot(pick_first, every).reshape(nrows, win_dev, parts_two, bins).astype(jnp.float32)
    second = (
        jnp.dot(pick_second, every).reshape(nrows, win_dev, parts_two, bins).astype(jnp.float32)
    )
    both = jnp.dot(pick_first, every_mask, preferred_element_type=jnp.float32) * jnp.dot(
        pick_second, every_mask, preferred_element_type=jnp.float32
    )
    count = jnp.maximum(jnp.sum(both, axis=1), 1.0)
    local = lax.dynamic_slice_in_dim(both, lax.axis_index("win") * win_dev, win_dev, 1)
    real_part = first[:, :, 0] * second[:, :, 0] + first[:, :, 1] * second[:, :, 1]
    imag_part = first[:, :, 1] * second[:, :, 0] - first[:, :, 0] * second[:, :, 1]
    stack = jnp.concatenate(
        [
            jnp.sum(local[:, :, None] * real_part, axis=1),
            jnp.sum(local[:, :, None] * imag_part, axis=1),
        ],
        axis=1,
    )
    return jnp.dot(stack, lag_table(bins, LAGS), precision=lax.Precision.HIGHEST) / count[:, None]


def body(spectra, masks, pairs, owners):
    sta_dev, win_dev, parts_two, bins = spectra.shape
    npair = pairs.shape[0]
    spec = spectra.astype(jnp.float32)
    power = jnp.mean(spec * spec, axis=(2, 3), keepdims=True)
    whitened = (spec * lax.rsqrt(power + 1e-05)).astype(jnp.bfloat16)
    flat = whitened.reshape(sta_dev, win_dev * parts_two * bins)
    valid = masks.astype(jnp.bfloat16)
    owner = owners[:, 0]
    later = lax.broadcasted_iota(jnp.int32, (npair, npair), 0)
    earlier = lax.broadcasted_iota(jnp.int32, (npair, npair), 1)
    same = (owner[:, None] == owner[None, :]) & (earlier < later)
    slot = jnp.sum(same.astype(jnp.int32), axis=1)
    peers = lax.axis_size("sta")
    capacity = 2 * npair // peers
    target = owner * capacity + slot
    rows = lax.broadcasted_iota(jnp.int32, (peers * capacity, npair), 0)
    selected = rows == target[None, :]
    every, every_mask = (
        lax.all_gather(flat, "sta", axis=0, tiled=True),
        lax.all_gather(valid, "sta", axis=0, tiled=True),
    )
    ones_live = jnp.ones((npair,), jnp.int32)
    correlogram = correlate(
        every, every_mask, pairs[:, 0], pairs[:, 1], ones_live, win_dev, parts_two, bins
    )
    dispatch = selected.astype(jnp.float32)
    outgoing = jnp.dot(dispatch, correlogram, precision=lax.Precision.HIGHEST)
    received = lax.all_to_all(outgoing, "sta", split_axis=0, concat_axis=0, tiled=True)
    stacks = lax.psum_scatter(received, "win", scatter_dimension=1, tiled=True)
    return stacks


def solution(mesh):
    placed = (P("sta", "win", None, None), P("sta", None), P("sta", None), P("sta", None))
    return jax.shard_map(
        body, mesh=mesh, in_specs=placed, out_specs=P("sta", "win"), check_vma=False
    )
```

profile of v0, /device:TPU:8, one launch (start us, length us, event | category | flops | bytes accessed | tf_op | source)
XLA Modules:
  0.0 187.9 jit_solution(107659116619828244)
XLA Ops:
  6.5 0.8 fusion.25
  7.4 0.8 fusion.26
  8.2 0.6 reshape.120
  8.8 0.0 reduce-scatter.2.cloned.1.call-start
  8.9 0.7 convert_bitcast_fusion
  9.6 49.2 %all-gather = bf16[128,2,4]{2,1,0:T(2,128)(2,1)S(1)} all-gather(bf16[1,2,4]{2,1,0:T(2,128)(2,1)S(1)} %convert_bitcast_fusion), channel_id=1, replica_groups=mesh['sta'=128,'win'=4] {'sta'}, dimensions={0}, use_global_device_ids=true | all-gather | bytes 2064 | tf_op jit(solution)/shard_map/all_gather | solution.py:69
  58.8 0.8 slice_bitcast_fusion
  59.5 0.2 fusion.17
  59.8 0.2 fusion.30
  60.0 0.9 convert_reduce_fusion
  60.9 0.7 multiply_add_fusion
  61.6 20.1 %cosine_multiply_fusion = (f32[2048,512]{1,0:T(8,128)}, f32[2048,512]{1,0:T(8,128)}) fusion(s32[512]{0:T(512)S(1)} %iota_add_fusion.1, s32[2048]{0:T(1024)S(1)} %iota_add_fusion), kind=kLoop, calls=%fused_computation.10 | loop fusion | flops 12582912 | bytes 8398848 | tf_op jit(solution)/shard_map/mul | solution.py:19
  81.7 15.7 %all-gather.4.cloned.1.call-done = bf16[128,2,4096]{2,1,0:T(2,128)(2,1)} async-done(((bf16[1,2,4096]{2,1,0:T(2,128)(2,1)}), bf16[128,2,4096]{2,1,0:T(2,128)(2,1)}) %all-gather.4.cloned.1.call-update) | async-done | bytes 2097168 | tf_op jit(solution)/shard_map/all_gather | solution.py:68
  97.5 2.7 %reshape.121 = bf16[256,4096]{1,0:T(8,128)(2,1)S(1)} reshape(bf16[128,2,4096]{2,1,0:T(2,128)(2,1)} %all-gather.4.cloned.1.call-done) | data formatting | bytes 4194304
  100.2 1.8 convolution_convert_fusion.1
  102.0 1.9 convolution_convert_fusion
  103.9 2.9 %copy.23 = f32[128,4096]{0,1:T(8,128)} copy(f32[128,4096]{1,0:T(8,128)} %convolution_convert_fusion.1) | data formatting | bytes 4194304 | tf_op jit(solution)/shard_map/convert_element_type | solution.py:28
  106.8 3.2 %fusion.29 = (f32[128,1,1,2048]{0,3,2,1:T(8,128)}, f32[128,1,1,2048]{0,3,2,1:T(8,128)}) fusion(f32[128,1,2,2048]{0,3,2,1:T(8,128)} %bitcast.22), kind=kLoop, calls=%fused_computation.50 | loop fusion | bytes 4194304 | tf_op jit(solution)/shard_map/slice | solution.py:37
  109.9 1.6 copy.29
  111.5 1.9 copy.25
  113.4 2.6 %fusion.28 = (f32[128,1,1,2048]{0,3,2,1:T(8,128)S(1)}, f32[128,1,1,2048]{0,3,2,1:T(8,128)}) fusion(f32[128,1,2,2048]{0,3,2,1:T(8,128)} %bitcast.23), kind=kLoop, calls=%fused_computation.49 | loop fusion | bytes 4194304 | tf_op jit(solution)/shard_map/slice | solution.py:37
  116.0 0.3 copy.30
  116.4 1.6 copy.31
  117.9 2.6 %copy.32 = f32[128,1,1,2048]{3,0,2,1:T(8,128)} copy(f32[128,1,1,2048]{0,3,2,1:T(8,128)} %get-tuple-element.8) | data formatting | bytes 2097152
  120.5 1.8 bitcast_multiply_fusion.1
  122.4 0.6 copy-done
  123.0 6.0 %fusion.12 = f32[128,512]{1,0:T(8,128)S(1)} fusion(f32[2048,512]{1,0:T(8,128)} %get-tuple-element.12, f32[2048,512]{1,0:T(8,128)S(1)} %copy-done, f32[128,2048]{1,0:T(8,128)S(1)} %get-tuple-element.6, f32[128,2048]{1,0:T(8,128)S(1)} %get-tuple-element.5, f32[128]{0:T(128)S(1)} %broadcast_maximum_fusion), kind=kOutput, calls=%fused_computation.21 | convolution fusion | flops 3223912448 | bytes 10748416 | tf_op jit(solution)/shard_map/dot_general | solution.py:46
  129.0 0.4 fusion.18
  129.4 0.3 all_to_all.8
  129.7 30.4 %all_to_all.12 = f32[128,2,512]{2,1,0:T(2,128)S(1)} all-to-all(f32[128,2,512]{2,1,0:T(2,128)S(1)} %all_to_all.8), channel_id=1, replica_groups=mesh['sta'=128,'win'=4] {'sta'}, dimensions={0} | all-to-all | bytes 1048576 | tf_op jit(solution)/shard_map/all_to_all | solution.py:77
  160.1 1.2 all_to_all.10
  161.3 19.8 %reduce-scatter.2.cloned.1.call-done = f32[256,128]{1,0:T(8,128)} async-done(((f32[256,512]{1,0:T(8,128)}), f32[256,128]{1,0:T(8,128)}) %reduce-scatter.2.cloned.1.call-update) | async-done | bytes 131088 | tf_op jit(solution)/shard_map/reduce_scatter | solution.py:78
  (11 shorter events, 0.1 us)
Async XLA Ops:
  6.5 90.9 %all-gather.4.cloned.1.call-start = ((), (), s32[]{:S(2)}) async-start(), calls=%async_computation.3 | async-start | bytes 2113536 | tf_op jit(solution)/shard_map/all_gather | solution.py:68
  8.8 172.3 %reduce-scatter.2.cloned.1.call-start = ((), (), s32[]{:S(2)}) async-start(), calls=%async_computation.2 | async-start | bytes 655360 | tf_op jit(solution)/shard_map/reduce_scatter | solution.py:78
  106.8 4.7 %copy-start.1 = (f32[128,4096]{1,0:T(8,128)S(1)}, f32[128,4096]{1,0:T(8,128)}, u32[]{:S(2)}) copy-start(f32[128,4096]{1,0:T(8,128)} %convolution_convert_fusion) | copy-start | bytes 6291460
  120.5 2.5 %copy-start = (f32[2048,512]{1,0:T(8,128)S(1)}, f32[2048,512]{1,0:T(8,128)}, u32[]{:S(2)}) copy-start(f32[2048,512]{1,0:T(8,128)} %get-tuple-element.11) | copy-start | bytes 12582916
Sparse Core Ops, SparseCore 0:
  10.5 86.9 all-gather.3
  161.4 19.6 reduce-scatter.1
where the time goes:
time: 188 us
  blocking collectives  79.6 us (42%)
  waiting for transfers between devices  35.5 us (19%)
  other arithmetic  25.9 us (14%)
  local copies, waits for them, and re-layouts  22.8 us (12%)
  between operations  13.5 us (7%)
  matrix products  10.5 us (6%)
    all_gather x1, blocking collectives, body(): lax.all_gather(valid, 'sta', axis=0, tiled=True)  49.2 us
    all_to_all x1, blocking collectives, body(): lax.all_to_all(outgoing, 'sta', split_axis=0, concat_axis=0, tiled=True)  30.4 us
    mul x1, other arithmetic, lag_table(): return jnp.concatenate([jnp.cos(angle) * scale, -jnp.sin(angle) * scale], 0)  20.1 us
    reduce_scatter x1, waiting for transfers between devices, body(): stacks = lax.psum_scatter(received, 'win', scatter_dimension=1, tiled=True)  19.8 us
    all_gather x1, waiting for transfers between devices, body(): lax.all_gather(flat, 'sta', axis=0, tiled=True)  15.7 us
    unnamed x10, local copies, waits for them, and re-layouts  10.1 us
    dot_general x1, matrix products, correlate(): jnp.dot(stack, lag_table(bins, LAGS), precision=lax.Precision.HIGHEST)  5.99 us
  transfers between devices with their start and end apart: 2, of which 2 were waited for; matrix products, arithmetic and copies ran while one was open for 13% of the time, Pallas kernels for 0%

commit v1 on v0

v1 whole, which is shorter than its diff:
```python
import functools
import math

import jax
import jax.numpy as jnp
import ml_dtypes
import numpy as np
from jax import lax
from jax.experimental import pallas as pl
from jax.experimental.pallas import tpu as pltpu
from jax.sharding import PartitionSpec as P

FIRST_BIN = 360
SAMPLES = 180000
MESH = pl.DeviceIdType.MESH
BF = jnp.bfloat16
F32 = jnp.float32
I32 = jnp.int32


def lag_tables(bins, lags):
    freq = np.arange(bins, dtype=np.int64)[:, None] + FIRST_BIN
    lag = np.arange(lags, dtype=np.int64)[None, :] - lags // 2
    angle = (freq * lag % SAMPLES).astype(np.float64) * (2.0 * math.pi / SAMPLES)
    scale = bins ** (-0.5)
    both = np.stack([np.cos(angle) * scale, -np.sin(angle) * scale]).astype(np.float32)
    both = both.reshape(2, 2, 2, bins // 4, lags).transpose(1, 2, 0, 3, 4)
    both = both.reshape(2, 2, bins // 2, lags)
    high = both.astype(ml_dtypes.bfloat16)
    low = (both - high.astype(np.float32)).astype(ml_dtypes.bfloat16)
    return np.stack([high, low], axis=2)


def iota(shape, dim):
    return lax.broadcasted_iota(I32, shape, dim)


def onehot(cond):
    return cond.astype(F32).astype(BF)


def dot(a, b):
    return jnp.dot(a, b, preferred_element_type=F32)


def kernel(
    Y, Z, X,
    spec_ref, list_ref, table_ref, out_ref,
    pka, pkb, p1a, p1b, every_a, every_b, lists, table, r1_out, r1_in, r2_out, r2_in,
    p1a_s, p1a_r, p1b_s, p1b_r, ring_s, ring_r, l2_s, l2_r, l3_s, l3_r, tab_sem,
    r1_s, r1_r, r2_s, r2_r,
):
    D = 2 * Y * Z
    NST = 2 * D
    GA, GB = 2 * Y, 2 * Z
    me = lax.axis_index("sta")
    x = lax.axis_index("win")
    y = me // (2 * Z)
    z = (me // 2) % Z
    c = me % 2
    sib = 1 - c

    def at(yy, zz, cc):
        return (yy * Z + zz) * 2 + cc

    barrier = pltpu.get_barrier_semaphore()

    def greet(sta, win):
        pl.semaphore_signal(barrier, inc=1, device_id=(sta, win), device_id_type=MESH)

    def greet_y(i, carry):
        greet(at((y + i) % Y, z, 0), x)
        greet(at((y + i) % Y, z, 1), x)
        return carry

    def greet_z(i, carry):
        greet(at(y, (z + i) % Z, 0), x)
        greet(at(y, (z + i) % Z, 1), x)
        return carry

    def greet_x(i, carry):
        greet(me, (x + i) % X)
        return carry

    greet(at(y, z, sib), x)
    lax.fori_loop(1, Y, greet_y, 0)
    lax.fori_loop(1, Z, greet_z, 0)
    lax.fori_loop(1, X, greet_x, 0)

    tab_copy = pltpu.make_async_copy(table_ref.at[c], table, tab_sem)
    tab_copy.start()

    bins = spec_ref.shape[3]
    J = bins // 512
    white = []
    for s in range(2):
        v = spec_ref[s, 0].astype(F32)
        power = jnp.sum(jnp.sum(v * v, axis=1, keepdims=True), axis=0, keepdims=True) * (
            1.0 / (2 * bins)
        )
        white.append(v * lax.rsqrt(power + 1e-05))
    for cc in range(2):
        for h, pk in ((0, pka), (1, pkb)):
            rows = []
            for s in range(2):
                for j in range(J):
                    start = (cc * 2 + h) * (bins // 4) + j * 128
                    rows.append(white[s][:, start : start + 128])
            pk[cc, 0 : 4 * J, :] = jnp.concatenate(rows, axis=0).astype(BF)
        pka[cc, 4 * J : 4 * J + 16, :] = list_ref[...]
    PR = 4 * J

    pl.semaphore_wait(barrier, 2 * (Y - 1) + 2 * (Z - 1) + 1 + X - 1)

    slot_a = y * 2 + c
    slot_b = z * 2 + c

    def send_a(yy, cc):
        pltpu.make_async_remote_copy(
            src_ref=pka.at[cc], dst_ref=p1a.at[slot_a], send_sem=p1a_s, recv_sem=p1a_r,
            device_id=(at(yy, z, cc), x), device_id_type=MESH,
        ).start()

    def send_b(zz, cc):
        pltpu.make_async_remote_copy(
            src_ref=pkb.at[cc], dst_ref=p1b.at[slot_b], send_sem=p1b_s, recv_sem=p1b_r,
            device_id=(at(y, zz, cc), x), device_id_type=MESH,
        ).start()

    def loop_a(i, carry):
        send_a((y + i) % Y, 0)
        send_a((y + i) % Y, 1)
        return carry

    def loop_b(i, carry):
        send_b((z + i) % Z, 0)
        send_b((z + i) % Z, 1)
        return carry

    lax.fori_loop(1, Y, loop_a, 0)
    lax.fori_loop(1, Z, loop_b, 0)
    send_a(y, sib)
    send_b(z, sib)
    p1a[slot_a] = pka[c]
    p1b[slot_b] = pkb[c]

    def relayout(group, size):
        n = iota((2 * J * size * 2, size * PR), 0)
        k = iota((2 * J * size * 2, size * PR), 1)
        st = n % (2 * size)
        rij = n // (2 * size)
        ri, j = rij // J, rij % J
        perm = onehot(k == (st // 2) * PR + (st % 2) * 2 * J + j * 2 + ri)
        return dot(perm, group).astype(BF)

    def wait_bytes(ref, sem):
        pltpu.make_async_copy(ref, ref, sem).wait()

    def neighbour(h, step):
        if h == 0:
            return at(y, (z + step + Z) % Z, c)
        return at((y + step + Y) % Y, z, c)

    def ring_copy(h, direction, step, sub):
        every = every_a if h == 0 else every_b
        size, pos = (Z, z) if h == 0 else (Y, y)
        sign = 1 if direction == 0 else -1
        block = (pos - sign * (step - 1) + 2 * size) % size
        half = every.shape[1] // 2
        view = every.at[block, pl.ds(sub * half, half)]
        return pltpu.make_async_remote_copy(
            src_ref=view, dst_ref=view,
            send_sem=ring_s.at[h, direction, step - 1, sub],
            recv_sem=ring_r.at[h, direction, step - 1, sub],
            device_id=(neighbour(h, sign), x), device_id_type=MESH,
        )

    def landed(h, direction, step, sub):
        every = every_a if h == 0 else every_b
        size, pos = (Z, z) if h == 0 else (Y, y)
        sign = 1 if direction == 0 else -1
        block = (pos - sign * step + 2 * size) % size
        half = every.shape[1] // 2
        view = every.at[block, pl.ds(sub * half, half)]
        return pltpu.make_async_remote_copy(
            src_ref=view, dst_ref=view,
            send_sem=ring_s.at[h, direction, step - 1, sub],
            recv_sem=ring_r.at[h, direction, step - 1, sub],
            device_id=(neighbour(h, sign), x), device_id_type=MESH,
        )

    def used(size, direction, step, sub):
        return step < size // 2 or (step == size // 2 and sub == direction)

    def ring_start(h, step):
        size = Z if h == 0 else Y
        for sub in range(2):
            for direction in range(2):
                if used(size, direction, step, sub):
                    if step > 1:
                        landed(h, direction, step - 1, sub).wait_recv()
                    ring_copy(h, direction, step, sub).start()

    def ring_drain(h):
        size = Z if h == 0 else Y
        for direction in range(2):
            for sub in range(2):
                for step in range(1, size // 2 + 1):
                    if used(size, direction, step, sub):
                        forwarded = step < size // 2 and used(size, direction, step + 1, sub)
                        if not forwarded:
                            landed(h, direction, step, sub).wait_recv()

    wait_bytes(p1a.at[pl.ds(0, GA - 1)], p1a_r)
    block = relayout(p1a[:, 0:PR, :].reshape(GA * PR, 128), GA)
    for q in range(2 * J):
        every_a[z, :, q * 128 : (q + 1) * 128] = block[q * 2 * GA : (q + 1) * 2 * GA]
    ring_start(0, 1)

    wait_bytes(p1b.at[pl.ds(0, GB - 1)], p1b_r)
    block = relayout(p1b[...].reshape(GB * PR, 128), GB)
    for q in range(2 * J):
        every_b[y, :, q * 128 : (q + 1) * 128] = block[q * 2 * GB : (q + 1) * 2 * GB]
    ring_start(1, 1)

    share = GA // X
    n = iota((4 * share, GA * 16), 0)
    k = iota((4 * share, GA * 16), 1)
    perm = onehot(k == (x * share + n % share) * 16 + n // share)
    lists[x, z] = dot(perm, p1a[:, PR : PR + 16, :].reshape(GA * 16, 128)).astype(BF)

    def list_z(i, carry):
        pltpu.make_async_remote_copy(
            src_ref=lists.at[x, z], dst_ref=lists.at[x, z], send_sem=l2_s, recv_sem=l2_r,
            device_id=(at(y, (z + i) % Z, c), x), device_id_type=MESH,
        ).start()
        return carry

    def list_x(i, carry):
        pltpu.make_async_remote_copy(
            src_ref=lists.at[x], dst_ref=lists.at[x], send_sem=l3_s, recv_sem=l3_r,
            device_id=(me, (x + i) % X), device_id_type=MESH,
        ).start()
        return carry

    lax.fori_loop(1, Z, list_z, 0)
    if Z // 2 >= 2:
        ring_start(0, 2)
    wait_bytes(lists.at[0, pl.ds(0, Z - 1)], l2_r)
    lax.fori_loop(1, X, list_x, 0)
    if Y // 2 >= 2:
        ring_start(1, 2)
    for step in range(3, max(Y, Z) // 2 + 1):
        if step <= Z // 2:
            ring_start(0, step)
        if step <= Y // 2:
            ring_start(1, step)

    if X > 1:
        wait_bytes(lists.at[pl.ds(0, X - 1)], l3_r)
    n = iota((4 * D, 4 * D), 0)
    k = iota((4 * D, 4 * D), 1)
    d = n % D
    q = n // D
    pos = (d // (2 * Z)) * 2 + d % 2
    src = ((pos // share) * Z + (d // 2) % Z) * (4 * share) + q * share + pos % share
    sorted_lists = dot(onehot(k == src), lists[...].reshape(4 * D, 128))
    first_id = sorted_lists[0:D]
    second_id = sorted_lists[D : 2 * D]
    owner_id = sorted_lists[2 * D : 3 * D]
    mask_rows = sorted_lists[3 * D : 4 * D].astype(BF)
    spread = onehot(iota((NST, D), 0) // 2 == iota((NST, D), 1))
    lane = iota((NST, 128), 1)
    mine = (lane // X == iota((NST, 128), 0) % 2) & (lane < 2 * X)
    fl, fw = iota((128, 128), 0), iota((128, 128), 1)
    fold = onehot((fl < 2 * X) & (fw < X) & (fl % X == fw))
    mask_st = dot(jnp.where(mine, dot(spread, mask_rows), 0.0).astype(BF), fold).astype(BF)
    tri = onehot(iota((128, 128), 0) < iota((128, 128), 1))
    ka = iota((2 * D, NST), 1)
    st_a = ((ka // 4) % Y) * (4 * Z) + (ka // (4 * Y)) * 4 + ka % 4
    st_a = st_a.astype(F32)
    st_b = ka.astype(F32)

    def slots_of(o):
        match = owner_id == o.astype(F32)
        mf = match.astype(F32)
        before = dot(mf.astype(BF), tri)
        picks = [mf * (before == float(i)).astype(F32) for i in range(2)]
        first = jnp.concatenate(
            [jnp.sum(p * (first_id + 1.0), axis=1, keepdims=True) for p in picks], axis=0
        ) - 1.0
        second = jnp.concatenate(
            [jnp.sum(p * (second_id + 1.0), axis=1, keepdims=True) for p in picks], axis=0
        ) - 1.0
        one_b = [onehot(st_b == first), onehot(st_b == second)]
        one_a = [onehot(st_a == first), onehot(st_a == second)]
        both = dot(one_b[0], mask_st) * dot(one_b[1], mask_st)
        count = jnp.maximum(jnp.sum(both, axis=1, keepdims=True), 1.0)
        here = jnp.where(iota(both.shape, 1) == x, both, 0.0)
        return one_a, one_b, jnp.sum(here, axis=1, keepdims=True) / count

    slots = [slots_of(me - c + sib), slots_of(me)]

    ring_drain(0)
    ring_drain(1)
    tab_copy.wait()

    def partial(which):
        one_a, one_b, scale = slots[which]
        quarter = bins // 4
        total = None
        for h, (ones, every) in enumerate(((one_a, every_a), (one_b, every_b))):
            stations = every[...].reshape(NST, 2 * quarter)
            f = dot(ones[0], stations)
            s = dot(ones[1], stations)
            fr, fi = f[:, :quarter], f[:, quarter:]
            sr, si = s[:, :quarter], s[:, quarter:]
            stack = jnp.concatenate([fr * sr + fi * si, fi * sr - fr * si], axis=1)
            high = stack.astype(BF)
            low = (stack - high.astype(F32)).astype(BF)
            part = dot(high, table[h, 0]) + (dot(high, table[h, 1]) + dot(low, table[h, 0]))
            total = part if total is None else total + part
        return total * scale

    r1_out[...] = partial(0)
    r1 = pltpu.make_async_remote_copy(
        src_ref=r1_out, dst_ref=r1_in, send_sem=r1_s, recv_sem=r1_r,
        device_id=(at(y, z, sib), x), device_id_type=MESH,
    )
    r1.start()
    own = partial(1)
    r1.wait_recv()
    own = own + r1_in[...]
    for xx in range(X):
        r2_out[xx] = own[:, xx * 128 : (xx + 1) * 128].astype(BF)
    r1_in[:, 0:128] = own[:, 0:128]
    for xx in range(1, X):
        @pl.when(x == xx)
        def _():
            r1_in[:, 0:128] = own[:, xx * 128 : (xx + 1) * 128]

    def r2_copy(i):
        return pltpu.make_async_remote_copy(
            src_ref=r2_out.at[(x + i) % X], dst_ref=r2_in.at[i], send_sem=r2_s.at[i],
            recv_sem=r2_r.at[i], device_id=(me, (x + i) % X), device_id_type=MESH,
        )

    for i in range(1, X):
        r2_copy(i).start()
    for i in range(1, X):
        r2_copy(i).wait_recv()
    result = r1_in[:, 0:128]
    for i in range(1, X):
        result = result + r2_in[i].astype(F32)
    out_ref[...] = result.reshape(2, D, 128)

    wait_bytes(p1a.at[pl.ds(0, GA - 1)], p1a_s)
    wait_bytes(p1b.at[pl.ds(0, GB - 1)], p1b_s)
    wait_bytes(lists.at[0, pl.ds(0, Z - 1)], l2_s)
    if X > 1:
        wait_bytes(lists.at[pl.ds(0, X - 1)], l3_s)
    for h, size in ((0, Z), (1, Y)):
        for step in range(1, size // 2 + 1):
            for direction in range(2):
                for sub in range(2):
                    if used(size, direction, step, sub):
                        ring_copy(h, direction, step, sub).wait_send()
    r1.wait_send()
    for i in range(1, X):
        r2_copy(i).wait_send()


def body(dims, spectra, masks, pairs, owners):
    Y, Z, X = dims
    bins = spectra.shape[3]
    lags = 128 * X
    D = 2 * Y * Z
    J = bins // 512
    PR = 4 * J
    flat_masks = jnp.pad(masks.reshape(1, 2 * X), ((0, 0), (0, 128 - 2 * X)))
    packet = jnp.concatenate([pairs.T, owners.T, flat_masks], axis=0)
    packet = jnp.pad(packet, ((0, 12), (0, 0))).astype(BF)
    table = jnp.asarray(lag_tables(bins, lags))
    dma = pltpu.SemaphoreType.DMA
    stacks = pl.pallas_call(
        functools.partial(kernel, Y, Z, X),
        out_shape=jax.ShapeDtypeStruct((2, D, 128), F32),
        in_specs=[
            pl.BlockSpec(memory_space=pltpu.VMEM),
            pl.BlockSpec(memory_space=pltpu.VMEM),
            pl.BlockSpec(memory_space=pl.ANY),
        ],
        out_specs=pl.BlockSpec(memory_space=pltpu.VMEM),
        scratch_shapes=[
            pltpu.VMEM((2, PR + 16, 128), BF),
            pltpu.VMEM((2, PR, 128), BF),
            pltpu.VMEM((2 * Y, PR + 16, 128), BF),
            pltpu.VMEM((2 * Z, PR, 128), BF),
            pltpu.VMEM((Z, 4 * Y, 2 * J * 128), BF),
            pltpu.VMEM((Y, 4 * Z, 2 * J * 128), BF),
            pltpu.VMEM((X, Z, 4 * (2 * Y // X), 128), BF),
            pltpu.VMEM((2, 2, bins // 2, lags), BF),
            pltpu.VMEM((2 * D, lags), F32),
            pltpu.VMEM((2 * D, lags), F32),
            pltpu.VMEM((X, 2 * D, 128), BF),
            pltpu.VMEM((X, 2 * D, 128), BF),
            dma, dma, dma, dma,
            dma((2, 2, max(Y, Z) // 2, 2)),
            dma((2, 2, max(Y, Z) // 2, 2)),
            dma, dma, dma, dma, dma,
            dma, dma, dma((X,)), dma((X,)),
        ],
        compiler_params=pltpu.CompilerParams(
            collective_id=0, has_side_effects=True, vmem_limit_bytes=48 * 1024 * 1024
        ),
    )(spectra, packet, table)
    return stacks.transpose(1, 0, 2).reshape(2 * D, 128)


def dims_of(mesh):
    sta, win = mesh.shape["sta"], mesh.shape["win"]
    side = math.isqrt(sta // 2)
    return side, sta // 2 // side, win


def solution(mesh):
    placed = (P("sta", "win", None, None), P("sta", None), P("sta", None), P("sta", None))
    return jax.shard_map(
        functools.partial(body, dims_of(mesh)),
        mesh=mesh, in_specs=placed, out_specs=P("sta", "win"), check_vma=False,
    )
```

time: 188 us -> 51.7 us (0.28)
  blocking collectives: 79.6 us -> 0 us
  Pallas kernels: 0 us -> 47.9 us
  waiting for transfers between devices: 35.5 us -> 0 us
  other arithmetic: 25.9 us -> 2.03 us
  local copies, waits for them, and re-layouts: 22.8 us -> 1.56 us
  between operations: 13.5 us -> 0.02 us
  matrix products: 10.5 us -> 0 us
    all_gather x1 -> x0, blocking collectives: 49.2 us -> none  [body(): lax.all_gather(valid, 'sta', axis=0, tiled=True)]
    pallas_call x0 -> x1, Pallas kernels: none -> 47.9 us  [body(): pl.pallas_call(functools.partial(kernel, Y, Z, X), out_shape=jax.ShapeDty...]
    all_to_all x1 -> x0, blocking collectives: 30.4 us -> none  [body(): lax.all_to_all(outgoing, 'sta', split_axis=0, concat_axis=0, tiled=True)]
    mul x2 -> x0, other arithmetic: 22 us -> none  [the longest x1 20.1 us: lag_table(): return jnp.concatenate([jnp.cos(angle) * scale, -jnp.sin(angle) * scale], 0)]
    reduce_scatter x1 -> x0, waiting for transfers between devices: 19.8 us -> none  [body(): stacks = lax.psum_scatter(received, 'win', scatter_dimension=1, tiled=True)]
    all_gather x1 -> x0, waiting for transfers between devices: 15.7 us -> none  [body(): lax.all_gather(flat, 'sta', axis=0, tiled=True)]
    dot_general x6 -> x0, matrix products: 10.5 us -> none  [the longest x1 5.99 us: correlate(): jnp.dot(stack, lag_table(bins, LAGS), precision=lax.Precision.HIGHEST)]
    unnamed x10 -> x2, local copies, waits for them, and re-layouts: 10.1 us -> 0.71 us
  transfers between devices with their start and end apart: 2 -> 0, of which waited for: 2 -> 0; matrix products, arithmetic and copies ran while one was open for 13% -> 0% of each run, Pallas kernels for 0% -> 0%
where the time goes in v1:
time: 51.7 us; the launch traced here: 51.5 us
  Pallas kernels  47.9 us (93%)
  other arithmetic  2.03 us (4%)
  local copies, waits for them, and re-layouts  1.56 us (3%)
    pallas_call x1, Pallas kernels, body(): pl.pallas_call(functools.partial(kernel, Y, Z, X), out_shape=jax.ShapeDty...  47.9 us
    transpose x2, other arithmetic, body(): packet = jnp.concatenate([pairs.T, owners.T, flat_masks], axis=0)  1.34 us

profile of v1, /device:TPU:8, one launch (start us, length us, event | category | flops | bytes accessed | tf_op | source)
XLA Modules:
  0.0 51.5 jit_solution(13621003371380281770)
XLA Ops:
  0.0 0.7 %convert.18 = bf16[2,4]{1,0:T(2,128)(2,1)S(1)} convert(s32[2,4]{1,0:T(2,128)} %param.6) | non-fusion elementwise | flops 8 | bytes 48 | tf_op jit(solution)/shard_map/convert.7
  0.7 0.1 reshape.7
  0.8 0.7 %convert_bitcast_fusion.1 = bf16[2,128]{1,0:T(2,128)(2,1)S(1)} fusion(s32[128,2]{0,1:T(2,128)} %param.7), kind=kLoop, calls=%fused_computation.4 | loop fusion | flops 256 | bytes 1536 | tf_op jit(solution)/shard_map/transpose | solution.py:381
  1.5 0.7 %convert_bitcast_fusion = bf16[1,128]{1,0:T(2,128)(2,1)S(1)} fusion(s32[128,1]{0,1:T(1,128)} %param.8), kind=kLoop, calls=%fused_computation.3 | loop fusion | flops 128 | bytes 768 | tf_op jit(solution)/shard_map/transpose | solution.py:381
  2.1 0.0 copy-start
  2.1 0.7 %copy-done = bf16[2,1,2,2048]{3,2,1,0:T(2,128)(2,1)S(1)} copy-done((bf16[2,1,2,2048]{3,2,1,0:T(2,128)(2,1)S(1)}, bf16[2,1,2,2048]{3,2,1,0:T(2,128)(2,1)}, u32[]{:S(2)}) %copy-start) | copy-done | bytes 16408
  2.9 47.9 %shard_map.55 = f32[2,128,128]{2,1,0:T(8,128)S(1)} custom-call(bf16[2,1,2,2048]{3,2,1,0:T(2,128)(2,1)S(1)} %copy-done, bf16[16,128]{1,0:T(8,128)(2,1)S(1)} %pad.11.list_ref, bf16[2,2,2,1024,512]{4,3,2,1,0:T(8,128)(2,1)} %constant.5.clone.table_ref), custom_call_target="tpu_custom_call" | custom-call | tf_op jit(solution)/shard_map/pallas_call | solution.py:385
  50.7 0.8 %copy.6 = f32[128,2,128]{2,1,0:T(2,128)} copy(f32[128,2,128]{2,0,1:T(8,128)S(1)} %bitcast.6) | data formatting | bytes 262144 | tf_op jit(solution)/shard_map/transpose | solution.py:417
  (2 shorter events, 0.0 us)
Async XLA Ops:
  2.1 0.7 %copy-start = (bf16[2,1,2,2048]{3,2,1,0:T(2,128)(2,1)S(1)}, bf16[2,1,2,2048]{3,2,1,0:T(2,128)(2,1)}, u32[]{:S(2)}) copy-start(bf16[2,1,2,2048]{3,2,1,0:T(2,128)(2,1)} %spec_ref.1) | copy-start | bytes 49156

commit v2 on v1

v2 whole, which is shorter than its diff:
```python
import functools
import math

import jax
import jax.numpy as jnp
import ml_dtypes
import numpy as np
from jax import lax
from jax.experimental import pallas as pl
from jax.experimental.pallas import tpu as pltpu
from jax.sharding import PartitionSpec as P

FIRST_BIN = 360
SAMPLES = 180000
WAVES = 2
MESH = pl.DeviceIdType.MESH
BF = jnp.bfloat16
F32 = jnp.float32
I32 = jnp.int32


def lag_tables(bins, lags):
    freq = np.arange(bins, dtype=np.int64)[:, None] + FIRST_BIN
    lag = np.arange(lags, dtype=np.int64)[None, :] - lags // 2
    angle = (freq * lag % SAMPLES).astype(np.float64) * (2.0 * math.pi / SAMPLES)
    scale = bins ** (-0.5)
    both = np.stack([np.cos(angle) * scale, -np.sin(angle) * scale]).astype(np.float32)
    both = both.reshape(2, 2, 2, WAVES, bins // 4 // WAVES, lags // 128, 128)
    both = both.transpose(1, 5, 2, 3, 0, 4, 6)
    both = both.reshape(2, lags // 128, 2, WAVES, bins // 2 // WAVES, 128)
    high = both.astype(ml_dtypes.bfloat16)
    low = (both - high.astype(np.float32)).astype(ml_dtypes.bfloat16)
    return np.stack([high, low], axis=4)


def iota(shape, dim):
    return lax.broadcasted_iota(I32, shape, dim)


def onehot(cond):
    return cond.astype(F32).astype(BF)


def dot(a, b):
    return jnp.dot(a, b, preferred_element_type=F32)


def div(a, n):
    return lax.shift_right_logical(a, jnp.full_like(a, n.bit_length() - 1))


def mod(a, n):
    return a & (n - 1)


def kernel(
    Y, Z, X,
    spec_hbm, mask_hbm, pair_hbm, owner_hbm, table_hbm, out_ref,
    spec_ref, mask_ref, pair_ref, owner_ref, table, perm_a, perm_b, perm_l,
    pka, pkb, p1a, p1b, every_a, every_b, lists, acc, r1_out, r1_in, r2_out, r2_in,
    in_sem, tab_sem, p1a_s, p1a_r, p1b_s, p1b_r, ring_s, ring_r, l2_s, l2_r, l3_s, l3_r,
    r1_s, r1_r, r2_s, r2_r,
):
    D = 2 * Y * Z
    NST = 2 * D
    GA, GB = 2 * Y, 2 * Z
    W = WAVES
    me = lax.axis_index("sta")
    x = lax.axis_index("win")
    y = me // (2 * Z)
    z = (me // 2) % Z
    c = me % 2
    sib = 1 - c

    def at(yy, zz, cc):
        return (yy * Z + zz) * 2 + cc

    inputs = [
        pltpu.make_async_copy(src, dst, in_sem.at[i])
        for i, (src, dst) in enumerate(
            ((spec_hbm, spec_ref), (pair_hbm, pair_ref), (owner_hbm, owner_ref), (mask_hbm, mask_ref))
        )
    ]
    for copy in inputs:
        copy.start()

    barrier = pltpu.get_barrier_semaphore()

    def greet(sta, win):
        pl.semaphore_signal(barrier, inc=1, device_id=(sta, win), device_id_type=MESH)

    def far_first(size):
        return sorted(range(1, size), key=lambda i: -min(i, size - i))

    for i in far_first(Y):
        for cc in range(2):
            greet(at((y + i) % Y, z, cc), x)
    for i in far_first(Z):
        for cc in range(2):
            greet(at(y, (z + i) % Z, cc), x)
    for i in far_first(X):
        greet(me, (x + i) % X)
    greet(at(y, z, sib), x)

    tab_copies = [
        pltpu.make_async_copy(table_hbm.at[c, (x + i) % X], table.at[i], tab_sem.at[i])
        for i in range(X)
    ]
    for copy in tab_copies:
        copy.start()

    bins = spec_ref.shape[3]
    J = bins // 512
    PR = 4 * J
    for copy in inputs:
        copy.wait()
    white = []
    for s in range(2):
        v = spec_ref[s, 0].astype(F32)
        power = jnp.sum(jnp.sum(v * v, axis=1, keepdims=True), axis=0, keepdims=True) * (
            1.0 / (2 * bins)
        )
        white.append(v * lax.rsqrt(power + 1e-05))
    lane = iota((1, 128), 1)
    mask_row = jnp.zeros((1, 128), F32)
    for s in range(2):
        for w in range(X):
            one = mask_ref[s : s + 1, w : w + 1].astype(F32)
            mask_row = jnp.where(lane == s * X + w, one, mask_row)
    packet = jnp.concatenate(
        [
            pair_ref[...].astype(F32), owner_ref[...].astype(F32), mask_row,
            jnp.zeros((12, 128), F32),
        ],
        axis=0,
    ).astype(BF)
    for cc in range(2):
        for h, pk in ((0, pka), (1, pkb)):
            rows = []
            for s in range(2):
                for j in range(J):
                    start = (cc * 2 + h) * (bins // 4) + j * 128
                    rows.append(white[s][:, start : start + 128])
            pk[cc, 0:PR, :] = jnp.concatenate(rows, axis=0).astype(BF)
        pka[cc, PR : PR + 16, :] = packet

    def relayout_perm(size):
        shape = (2 * J * size * 2, size * PR)
        n, k = iota(shape, 0), iota(shape, 1)
        st, rij = mod(n, 2 * size), div(n, 2 * size)
        ri, j = div(rij, J), mod(rij, J)
        return onehot(k == div(st, 2) * PR + mod(st, 2) * 2 * J + j * 2 + ri)

    perm_a[...] = relayout_perm(GA)
    perm_b[...] = relayout_perm(GB)
    share = GA // X
    n, k = iota((4 * share, GA * 16), 0), iota((4 * share, GA * 16), 1)
    perm_l[...] = onehot(k == (x * share + mod(n, share)) * 16 + div(n, share))

    pl.semaphore_wait(barrier, 2 * (Y - 1) + 2 * (Z - 1) + 1 + X - 1)

    slot_a = y * 2 + c
    slot_b = z * 2 + c

    def send_a(yy, cc):
        pltpu.make_async_remote_copy(
            src_ref=pka.at[cc], dst_ref=p1a.at[slot_a], send_sem=p1a_s, recv_sem=p1a_r,
            device_id=(at(yy, z, cc), x), device_id_type=MESH,
        ).start()

    def send_b(zz, cc):
        pltpu.make_async_remote_copy(
            src_ref=pkb.at[cc], dst_ref=p1b.at[slot_b], send_sem=p1b_s, recv_sem=p1b_r,
            device_id=(at(y, zz, cc), x), device_id_type=MESH,
        ).start()

    for i in far_first(Y):
        for cc in range(2):
            send_a((y + i) % Y, cc)
    send_a(y, sib)
    for i in far_first(Z):
        for cc in range(2):
            send_b((z + i) % Z, cc)
    send_b(z, sib)
    p1a[slot_a] = pka[c]
    p1b[slot_b] = pkb[c]

    def wait_bytes(ref, sem):
        pltpu.make_async_copy(ref, ref, sem).wait()

    def hop(h, w, direction, dist):
        every, size, pos = ((every_a, Z, z), (every_b, Y, y))[h]
        sign = 1 - 2 * direction
        parent = 2 if dist > 2 else 0
        to = (pos + sign * (dist - parent) + size) % size
        rows = every.shape[2]

        def view(block):
            if 2 * dist == size:
                return every.at[w, block, pl.ds(direction * (rows // 2), rows // 2)]
            return every.at[w, block]

        sent = view((pos - sign * parent + size) % size)
        comes = view((pos - sign * dist + size) % size)
        sems = (ring_s.at[h, w, direction, dist - 1], ring_r.at[h, w, direction, dist - 1])
        dev = (at(y, to, c) if h == 0 else at(to, z, c), x)
        out, arrive = (
            pltpu.make_async_remote_copy(
                src_ref=v, dst_ref=v, send_sem=sems[0], recv_sem=sems[1],
                device_id=dev, device_id_type=MESH,
            )
            for v in (sent, comes)
        )
        return out, arrive

    half_way = (Z // 2, Y // 2)

    def start_direct(h):
        for w in range(W):
            for dist in range(1, min(2, half_way[h]) + 1):
                for direction in range(2):
                    hop(h, w, direction, dist)[0].start()

    def forward(h, w):
        if half_way[h] > 2:
            for direction in range(2):
                hop(h, w, direction, 2)[1].wait_recv()
                for dist in range(3, half_way[h] + 1):
                    hop(h, w, direction, dist)[0].start()

    def drain(h, w):
        for dist in range(1, half_way[h] + 1):
            if dist == 2 and half_way[h] > 2:
                continue
            for direction in range(2):
                hop(h, w, direction, dist)[1].wait_recv()

    jw = J // W

    def place(every, pos, perm, group, size):
        block = dot(perm[...], group).astype(BF)
        for w in range(W):
            for ri in range(2):
                for j in range(jw):
                    row = (ri * J + w * jw + j) * 2 * size
                    col = (ri * jw + j) * 128
                    every[w, pos, :, col : col + 128] = block[row : row + 2 * size]

    wait_bytes(p1a.at[pl.ds(0, GA - 1)], p1a_r)

    lists[x, z] = dot(perm_l[...], p1a[:, PR : PR + 16, :].reshape(GA * 16, 128)).astype(BF)
    for i in far_first(Z):
        pltpu.make_async_remote_copy(
            src_ref=lists.at[x, z], dst_ref=lists.at[x, z], send_sem=l2_s, recv_sem=l2_r,
            device_id=(at(y, (z + i) % Z, c), x), device_id_type=MESH,
        ).start()

    place(every_a, z, perm_a, p1a[:, 0:PR, :].reshape(GA * PR, 128), GA)
    start_direct(0)
    wait_bytes(p1b.at[pl.ds(0, GB - 1)], p1b_r)
    place(every_b, y, perm_b, p1b[...].reshape(GB * PR, 128), GB)
    start_direct(1)

    forward(0, 0)
    forward(1, 0)
    if Z > 1:
        wait_bytes(lists.at[0, pl.ds(0, Z - 1)], l2_r)
    for i in far_first(X):
        pltpu.make_async_remote_copy(
            src_ref=lists.at[x], dst_ref=lists.at[x], send_sem=l3_s, recv_sem=l3_r,
            device_id=(me, (x + i) % X), device_id_type=MESH,
        ).start()
    for w in range(1, W):
        forward(0, w)
        forward(1, w)

    n, k = iota((4 * D, 4 * D), 0), iota((4 * D, 4 * D), 1)
    d, q = mod(n, D), div(n, D)
    pos = div(d, 2 * Z) * 2 + mod(d, 2)
    src = (div(pos, share) * Z + mod(div(d, 2), Z)) * (4 * share) + q * share + mod(pos, share)
    perm = onehot(k == src)
    if X > 1:
        wait_bytes(lists.at[pl.ds(0, X - 1)], l3_r)
    sorted_lists = dot(perm, lists[...].reshape(4 * D, 128))
    first_id = sorted_lists[0:D]
    second_id = sorted_lists[D : 2 * D]
    owner_id = sorted_lists[2 * D : 3 * D]
    mask_rows = sorted_lists[3 * D : 4 * D].astype(BF)
    spread = onehot(div(iota((NST, D), 0), 2) == iota((NST, D), 1))
    lane = iota((NST, 128), 1)
    mine = (div(lane, X) == mod(iota((NST, 128), 0), 2)) & (lane < 2 * X)
    fl, fw = iota((128, 128), 0), iota((128, 128), 1)
    fold = onehot((fl < 2 * X) & (fw < X) & (mod(fl, X) == fw))
    mask_st = dot(jnp.where(mine, dot(spread, mask_rows), 0.0).astype(BF), fold).astype(BF)
    tri = onehot(iota((128, 128), 0) < iota((128, 128), 1))
    ka = iota((2 * D, NST), 1)
    st_a = mod(div(ka, 4), Y) * (4 * Z) + div(ka, 4 * Y) * 4 + mod(ka, 4)
    st_a = st_a.astype(F32)
    st_b = ka.astype(F32)

    def slots_of(o):
        match = owner_id == o.astype(F32)
        mf = match.astype(F32)
        before = dot(mf.astype(BF), tri)
        picks = [mf * (before == float(i)).astype(F32) for i in range(2)]
        first = jnp.concatenate(
            [jnp.sum(p * (first_id + 1.0), axis=1, keepdims=True) for p in picks], axis=0
        ) - 1.0
        second = jnp.concatenate(
            [jnp.sum(p * (second_id + 1.0), axis=1, keepdims=True) for p in picks], axis=0
        ) - 1.0
        one_b = [onehot(st_b == first), onehot(st_b == second)]
        one_a = [onehot(st_a == first), onehot(st_a == second)]
        both = dot(one_b[0], mask_st) * dot(one_b[1], mask_st)
        count = jnp.maximum(jnp.sum(both, axis=1, keepdims=True), 1.0)
        here = jnp.where(iota(both.shape, 1) == x, both, 0.0)
        return (one_a, one_b), jnp.sum(here, axis=1, keepdims=True) / count

    slots = [slots_of(me - c + sib), slots_of(me)]
    for copy in tab_copies:
        copy.wait()

    if X == 4:
        sides = ((2, 1), (3, 0))
    elif X == 2:
        sides = ((1,), (0,))
    else:
        sides = ((0,),)
    quarter = bins // 4 // W

    def stack_of(which, w):
        parts = []
        for h, every in enumerate((every_a, every_b)):
            ones = slots[which][0][h]
            stations = every[w].reshape(NST, 2 * quarter)
            f = dot(ones[0], stations)
            s = dot(ones[1], stations)
            fr, fi = f[:, :quarter], f[:, quarter:]
            sr, si = s[:, :quarter], s[:, quarter:]
            stack = jnp.concatenate([fr * sr + fi * si, fi * sr - fr * si], axis=1)
            high = stack.astype(BF)
            low = (stack - high.astype(F32)).astype(BF)
            parts.append((high, low))
        return parts

    def product(parts, w, side):
        total = None
        for h, (high, low) in enumerate(parts):
            t_high, t_low = (
                jnp.concatenate([table[i, h, w, p] for i in sides[side]], axis=1)
                for p in range(2)
            )
            part = dot(high, t_high) + (dot(high, t_low) + dot(low, t_high))
            total = part if total is None else total + part
        return total

    NS = len(sides)
    wide = 128 * len(sides[0])
    for w in range(W - 1):
        drain(0, w)
        drain(1, w)
        for which in range(2):
            parts = stack_of(which, w)
            for side in range(NS):
                value = product(parts, w, side)
                if w > 0:
                    value = value + acc[which, side]
                acc[which, side] = value
    w = W - 1
    drain(0, w)
    drain(1, w)

    def finish(which, side, parts):
        value = product(parts, w, side)
        if W > 1:
            value = value + acc[which, side]
        return value * slots[which][1]

    def r1_copy(side):
        return pltpu.make_async_remote_copy(
            src_ref=r1_out.at[side], dst_ref=r1_in.at[side], send_sem=r1_s.at[side],
            recv_sem=r1_r.at[side], device_id=(at(y, z, sib), x), device_id_type=MESH,
        )

    def r2_copy(i):
        return pltpu.make_async_remote_copy(
            src_ref=r2_out.at[i], dst_ref=r2_in.at[i], send_sem=r2_s.at[i],
            recv_sem=r2_r.at[i], device_id=(me, (x + i) % X), device_id_type=MESH,
        )

    parts = stack_of(0, w)
    for side in range(NS):
        r1_out[side] = finish(0, side, parts)
        r1_copy(side).start()
    parts = stack_of(1, w)
    for side in range(NS):
        acc[1, side] = finish(1, side, parts)
    for side in range(NS):
        r1_copy(side).wait_recv()
        for m, i in enumerate(sides[side]):
            piece = acc[1, side, :, m * 128 : (m + 1) * 128] + r1_in[side, :, m * 128 : (m + 1) * 128]
            if i > 0:
                r2_out[i] = piece.astype(BF)
                r2_copy(i).start()
            else:
                result = piece
    for i in range(1, X):
        r2_copy(i).wait_recv()
        result = result + r2_in[i].astype(F32)
    out_ref[...] = result.reshape(2, D, 128)

    wait_bytes(p1a.at[pl.ds(0, GA - 1)], p1a_s)
    wait_bytes(p1b.at[pl.ds(0, GB - 1)], p1b_s)
    if Z > 1:
        wait_bytes(lists.at[0, pl.ds(0, Z - 1)], l2_s)
    if X > 1:
        wait_bytes(lists.at[pl.ds(0, X - 1)], l3_s)
    for h in range(2):
        for w in range(W):
            for direction in range(2):
                for dist in range(1, half_way[h] + 1):
                    hop(h, w, direction, dist)[0].wait_send()
    for side in range(NS):
        r1_copy(side).wait_send()
    for i in range(1, X):
        r2_copy(i).wait_send()


def body(dims, spectra, masks, pairs, owners):
    Y, Z, X = dims
    bins = spectra.shape[3]
    lags = 128 * X
    D = 2 * Y * Z
    J = bins // 512
    PR = 4 * J
    W = WAVES
    table = jnp.asarray(lag_tables(bins, lags))
    sides = 2 if X > 1 else 1
    wide = lags // sides
    dma = pltpu.SemaphoreType.DMA
    stacks = pl.pallas_call(
        functools.partial(kernel, Y, Z, X),
        out_shape=jax.ShapeDtypeStruct((2, D, 128), F32),
        in_specs=[pl.BlockSpec(memory_space=pl.ANY)] * 5,
        out_specs=pl.BlockSpec(memory_space=pltpu.VMEM),
        scratch_shapes=[
            pltpu.VMEM(spectra.shape, BF),
            pltpu.VMEM(masks.shape, I32),
            pltpu.VMEM((2, 128), I32),
            pltpu.VMEM((1, 128), I32),
            pltpu.VMEM(table.shape[1:], BF),
            pltpu.VMEM((8 * J * Y, 2 * Y * PR), BF),
            pltpu.VMEM((8 * J * Z, 2 * Z * PR), BF),
            pltpu.VMEM((4 * (2 * Y // X), 2 * Y * 16), BF),
            pltpu.VMEM((2, PR + 16, 128), BF),
            pltpu.VMEM((2, PR, 128), BF),
            pltpu.VMEM((2 * Y, PR + 16, 128), BF),
            pltpu.VMEM((2 * Z, PR, 128), BF),
            pltpu.VMEM((W, Z, 4 * Y, 2 * J * 128 // W), BF),
            pltpu.VMEM((W, Y, 4 * Z, 2 * J * 128 // W), BF),
            pltpu.VMEM((X, Z, 4 * (2 * Y // X), 128), BF),
            pltpu.VMEM((2, sides, 2 * D, wide), F32),
            pltpu.VMEM((sides, 2 * D, wide), F32),
            pltpu.VMEM((sides, 2 * D, wide), F32),
            pltpu.VMEM((X, 2 * D, 128), BF),
            pltpu.VMEM((X, 2 * D, 128), BF),
            dma((4,)), dma((X,)), dma, dma, dma, dma,
            dma((2, W, 2, max(Y, Z) // 2)),
            dma((2, W, 2, max(Y, Z) // 2)),
            dma, dma, dma, dma,
            dma((sides,)), dma((sides,)), dma((X,)), dma((X,)),
        ],
        compiler_params=pltpu.CompilerParams(
            collective_id=0, has_side_effects=True, vmem_limit_bytes=48 * 1024 * 1024
        ),
    )(spectra, masks, pairs.T, owners.T, table)
    return stacks.transpose(1, 0, 2).reshape(2 * D, 128)


def dims_of(mesh):
    sta, win = mesh.shape["sta"], mesh.shape["win"]
    side = math.isqrt(sta // 2)
    return side, sta // 2 // side, win


def solution(mesh):
    placed = (P("sta", "win", None, None), P("sta", None), P("sta", None), P("sta", None))
    return jax.shard_map(
        functools.partial(body, dims_of(mesh)),
        mesh=mesh, in_specs=placed, out_specs=P("sta", "win"), check_vma=False,
    )
```

time: 51.7 us -> 45.4 us (0.88)
  Pallas kernels: 47.9 us -> 41.7 us
  other arithmetic: 2.03 us -> 0 us
  local copies, waits for them, and re-layouts: 1.56 us -> 3.49 us
    pallas_call x1, Pallas kernels: 47.9 us -> 41.7 us  [body(): pl.pallas_call(functools.partial(kernel, Y, Z, X), out_shape=jax.ShapeDty...]
    unnamed x2 -> x8, local copies, waits for them, and re-layouts: 0.71 us -> 2.73 us
    transpose x2 -> x0, other arithmetic: 1.34 us -> none  [body(): packet = jnp.concatenate([pairs.T, owners.T, flat_masks], axis=0)]
    another operation x1 -> x0, other arithmetic: 0.68 us -> none
where the time goes in v2:
time: 45.4 us; the launch traced here: 45.2 us
  Pallas kernels  41.7 us (92%)
  local copies, waits for them, and re-layouts  3.49 us (8%)
    pallas_call x1, Pallas kernels, body(): pl.pallas_call(functools.partial(kernel, Y, Z, X), out_shape=jax.ShapeDty...  41.7 us
    unnamed x8, local copies, waits for them, and re-layouts  2.73 us

profile of v2, /device:TPU:8, one launch (start us, length us, event | category | flops | bytes accessed | tf_op | source)
XLA Modules:
  0.0 45.2 jit_solution(13674117609814246919)
XLA Ops:
  0.0 0.0 copy-start
  0.0 0.7 %copy-done = bf16[2,1,2,2048]{3,2,1,0:T(2,128)(2,1)S(1)} copy-done((bf16[2,1,2,2048]{3,2,1,0:T(2,128)(2,1)S(1)}, bf16[2,1,2,2048]{3,2,1,0:T(2,128)(2,1)}, u32[]{:S(2)}) %copy-start) | copy-done | bytes 16408
  0.7 0.0 copy-start.1
  0.7 0.7 %copy-done.1 = s32[2,4]{1,0:T(2,128)S(1)} copy-done((s32[2,4]{1,0:T(2,128)S(1)}, s32[2,4]{1,0:T(2,128)}, u32[]{:S(2)}) %copy-start.1) | copy-done | bytes 56
  1.4 0.0 copy-start.2
  1.4 0.7 %copy-done.2 = s32[128,2]{0,1:T(2,128)S(1)} copy-done((s32[128,2]{0,1:T(2,128)S(1)}, s32[128,2]{0,1:T(2,128)}, u32[]{:S(2)}) %copy-start.2) | copy-done | bytes 1048
  2.1 0.0 copy-start.3
  2.1 0.7 %copy-done.3 = s32[128,1]{0,1:T(1,128)S(1)} copy-done((s32[128,1]{0,1:T(1,128)S(1)}, s32[128,1]{0,1:T(1,128)}, u32[]{:S(2)}) %copy-start.3) | copy-done | bytes 536
  2.7 41.7 %shard_map.55 = f32[2,128,128]{2,1,0:T(8,128)S(1)} custom-call(bf16[2,1,2,2048]{3,2,1,0:T(2,128)(2,1)S(1)} %copy-done, s32[2,4]{1,0:T(2,128)S(1)} %copy-done.1, s32[2,128]{1,0:T(2,128)S(1)} %bitcast.5, s32[1,128]{1,0:T(1,128)S(1)} %bitcast.6, bf16[2,4,2,2,2,512,128]{6,5,4,3,2,1,0:T(8,128)(2,1)} %constant.2.clone.table_hbm), custom_call_target="tpu_custom_call" | custom-call | tf_op jit(solution)/shard_map/pallas_call | solution.py:441
  44.4 0.8 %copy.6 = f32[128,2,128]{2,1,0:T(2,128)} copy(f32[128,2,128]{2,0,1:T(8,128)S(1)} %bitcast.4) | data formatting | bytes 262144 | tf_op jit(solution)/shard_map/transpose | solution.py:477
Async XLA Ops:
  0.0 0.7 %copy-start = (bf16[2,1,2,2048]{3,2,1,0:T(2,128)(2,1)S(1)}, bf16[2,1,2,2048]{3,2,1,0:T(2,128)(2,1)}, u32[]{:S(2)}) copy-start(bf16[2,1,2,2048]{3,2,1,0:T(2,128)(2,1)} %spec_hbm.1) | copy-start | bytes 49156
  0.7 0.7 %copy-start.1 = (s32[2,4]{1,0:T(2,128)S(1)}, s32[2,4]{1,0:T(2,128)}, u32[]{:S(2)}) copy-start(s32[2,4]{1,0:T(2,128)} %mask_hbm.1) | copy-start | bytes 100
  1.4 0.7 %copy-start.2 = (s32[128,2]{0,1:T(2,128)S(1)}, s32[128,2]{0,1:T(2,128)}, u32[]{:S(2)}) copy-start(s32[128,2]{0,1:T(2,128)} %param.7) | copy-start | bytes 3076
  2.1 0.7 %copy-start.3 = (s32[128,1]{0,1:T(1,128)S(1)}, s32[128,1]{0,1:T(1,128)}, u32[]{:S(2)}) copy-start(s32[128,1]{0,1:T(1,128)} %param.8) | copy-start | bytes 1540

commit v3 on v2

--- a/solution.py
+++ b/solution.py
@@ -56,7 +56,7 @@
 def kernel(
     Y, Z, X,
     spec_hbm, mask_hbm, pair_hbm, owner_hbm, table_hbm, out_ref,
-    spec_ref, mask_ref, pair_ref, owner_ref, table, perm_a, perm_b, perm_l,
+    spec_ref, mask_ref, pair_ref, owner_ref, table, perm_a, perm_b, perm_l, perm_s,
     pka, pkb, p1a, p1b, every_a, every_b, lists, acc, r1_out, r1_in, r2_out, r2_in,
     in_sem, tab_sem, p1a_s, p1a_r, p1b_s, p1b_r, ring_s, ring_r, l2_s, l2_r, l3_s, l3_r,
     r1_s, r1_r, r2_s, r2_r,
@@ -101,13 +101,6 @@
     for i in far_first(X):
         greet(me, (x + i) % X)
     greet(at(y, z, sib), x)
-
-    tab_copies = [
-        pltpu.make_async_copy(table_hbm.at[c, (x + i) % X], table.at[i], tab_sem.at[i])
-        for i in range(X)
-    ]
-    for copy in tab_copies:
-        copy.start()
 
     bins = spec_ref.shape[3]
     J = bins // 512
@@ -151,12 +144,6 @@
         ri, j = div(rij, J), mod(rij, J)
         return onehot(k == div(st, 2) * PR + mod(st, 2) * 2 * J + j * 2 + ri)
 
-    perm_a[...] = relayout_perm(GA)
-    perm_b[...] = relayout_perm(GB)
-    share = GA // X
-    n, k = iota((4 * share, GA * 16), 0), iota((4 * share, GA * 16), 1)
-    perm_l[...] = onehot(k == (x * share + mod(n, share)) * 16 + div(n, share))
-
     pl.semaphore_wait(barrier, 2 * (Y - 1) + 2 * (Z - 1) + 1 + X - 1)
 
     slot_a = y * 2 + c
@@ -184,6 +171,19 @@
     send_b(z, sib)
     p1a[slot_a] = pka[c]
     p1b[slot_b] = pkb[c]
+
+    tab_copies = [
+        pltpu.make_async_copy(table_hbm.at[c, (x + i) % X], table.at[i], tab_sem.at[i])
+        for i in range(X)
+    ]
+    for copy in tab_copies:
+        copy.start()
+
+    perm_a[...] = relayout_perm(GA)
+    perm_b[...] = relayout_perm(GB)
+    share = GA // X
+    n, k = iota((4 * share, GA * 16), 0), iota((4 * share, GA * 16), 1)
+    perm_l[...] = onehot(k == (x * share + mod(n, share)) * 16 + div(n, share))
 
     def wait_bytes(ref, sem):
         pltpu.make_async_copy(ref, ref, sem).wait()
@@ -217,9 +217,10 @@
 
     def start_direct(h):
         for w in range(W):
-            for dist in range(1, min(2, half_way[h]) + 1):
-                for direction in range(2):
-                    hop(h, w, direction, dist)[0].start()
+            for dist in (2, 1):
+                if dist <= half_way[h]:
+                    for direction in range(2):
+                        hop(h, w, direction, dist)[0].start()
 
     def forward(h, w):
         if half_way[h] > 2:
@@ -248,40 +249,49 @@
 
     wait_bytes(p1a.at[pl.ds(0, GA - 1)], p1a_r)
 
-    lists[x, z] = dot(perm_l[...], p1a[:, PR : PR + 16, :].reshape(GA * 16, 128)).astype(BF)
-    for i in far_first(Z):
-        pltpu.make_async_remote_copy(
-            src_ref=lists.at[x, z], dst_ref=lists.at[x, z], send_sem=l2_s, recv_sem=l2_r,
-            device_id=(at(y, (z + i) % Z, c), x), device_id_type=MESH,
-        ).start()
+    def lists_x():
+        if Z > 1:
+            wait_bytes(lists.at[0, pl.ds(0, Z - 1)], l2_r)
+        for i in far_first(X):
+            pltpu.make_async_remote_copy(
+                src_ref=lists.at[x], dst_ref=lists.at[x], send_sem=l3_s, recv_sem=l3_r,
+                device_id=(me, (x + i) % X), device_id_type=MESH,
+            ).start()
+
+    def prepare():
+        n, k = iota((4 * D, 4 * D), 0), iota((4 * D, 4 * D), 1)
+        d, q = mod(n, D), div(n, D)
+        pos = div(d, 2 * Z) * 2 + mod(d, 2)
+        src = (div(pos, share) * Z + mod(div(d, 2), Z)) * (4 * share) + q * share + mod(pos, share)
+        perm_s[...] = onehot(k == src)
+
+    def lists_z():
+        lists[x, z] = dot(perm_l[...], p1a[:, PR : PR + 16, :].reshape(GA * 16, 128)).astype(BF)
+        for i in far_first(Z):
+            pltpu.make_async_remote_copy(
+                src_ref=lists.at[x, z], dst_ref=lists.at[x, z], send_sem=l2_s, recv_sem=l2_r,
+                device_id=(at(y, (z + i) % Z, c), x), device_id_type=MESH,
+            ).start()
+
+    lists_z()
 
     place(every_a, z, perm_a, p1a[:, 0:PR, :].reshape(GA * PR, 128), GA)
     start_direct(0)
     wait_bytes(p1b.at[pl.ds(0, GB - 1)], p1b_r)
     place(every_b, y, perm_b, p1b[...].reshape(GB * PR, 128), GB)
     start_direct(1)
+    prepare()
+    lists_x()
 
     forward(0, 0)
     forward(1, 0)
-    if Z > 1:
-        wait_bytes(lists.at[0, pl.ds(0, Z - 1)], l2_r)
-    for i in far_first(X):
-        pltpu.make_async_remote_copy(
-            src_ref=lists.at[x], dst_ref=lists.at[x], send_sem=l3_s, recv_sem=l3_r,
-            device_id=(me, (x + i) % X), device_id_type=MESH,
-        ).start()
     for w in range(1, W):
         forward(0, w)
         forward(1, w)
 
-    n, k = iota((4 * D, 4 * D), 0), iota((4 * D, 4 * D), 1)
-    d, q = mod(n, D), div(n, D)
-    pos = div(d, 2 * Z) * 2 + mod(d, 2)
-    src = (div(pos, share) * Z + mod(div(d, 2), Z)) * (4 * share) + q * share + mod(pos, share)
-    perm = onehot(k == src)
     if X > 1:
         wait_bytes(lists.at[pl.ds(0, X - 1)], l3_r)
-    sorted_lists = dot(perm, lists[...].reshape(4 * D, 128))
+    sorted_lists = dot(perm_s[...], lists[...].reshape(4 * D, 128))
     first_id = sorted_lists[0:D]
     second_id = sorted_lists[D : 2 * D]
     owner_id = sorted_lists[2 * D : 3 * D]
@@ -452,6 +462,7 @@
             pltpu.VMEM((8 * J * Y, 2 * Y * PR), BF),
             pltpu.VMEM((8 * J * Z, 2 * Z * PR), BF),
             pltpu.VMEM((4 * (2 * Y // X), 2 * Y * 16), BF),
+            pltpu.VMEM((4 * D, 4 * D), BF),
             pltpu.VMEM((2, PR + 16, 128), BF),
             pltpu.VMEM((2, PR, 128), BF),
             pltpu.VMEM((2 * Y, PR + 16, 128), BF),
@@ -471,7 +482,7 @@
             dma((sides,)), dma((sides,)), dma((X,)), dma((X,)),
         ],
         compiler_params=pltpu.CompilerParams(
-            collective_id=0, has_side_effects=True, vmem_limit_bytes=48 * 1024 * 1024
+            collective_id=0, has_side_effects=True, vmem_limit_bytes=63 * 1024 * 1024
         ),
     )(spectra, masks, pairs.T, owners.T, table)
     return stacks.transpose(1, 0, 2).reshape(2 * D, 128)

time: 45.4 us -> 43.8 us (0.965)
  the two profiles are of different devices: /device:TPU:8 before, /device:TPU:3 now
where the time goes in v3:
time: 43.8 us; the launch traced here: 43.6 us
  Pallas kernels  42 us (96%)
  local copies, waits for them, and re-layouts  1.66 us (4%)
    pallas_call x1, Pallas kernels, body(): pl.pallas_call(functools.partial(kernel, Y, Z, X), out_shape=jax.ShapeDty...  42 us
    transpose x1, local copies, waits for them, and re-layouts, body(): return stacks.transpose(1, 0, 2).reshape(2 * D, 128)  1.66 us

profile of v3, /device:TPU:3, one launch (start us, length us, event | category | flops | bytes accessed | tf_op | source)
XLA Modules:
  0.0 43.6 jit_solution(9986005479827717269)
XLA Ops:
  0.0 42.0 %shard_map.55 = f32[2,128,128]{2,1,0:T(8,128)} custom-call(bf16[2,1,2,2048]{3,2,1,0:T(2,128)(2,1)} %spec_hbm.1, s32[2,4]{1,0:T(2,128)} %mask_hbm.1, s32[2,128]{1,0:T(2,128)} %bitcast.5, s32[1,128]{1,0:T(1,128)} %bitcast.6, bf16[2,4,2,2,2,512,128]{6,5,4,3,2,1,0:T(8,128)(2,1)} %constant.2.clone.table_hbm), custom_call_target="tpu_custom_call" | custom-call | tf_op jit(solution)/shard_map/pallas_call | solution.py:451
  42.0 1.7 %copy.6 = f32[128,2,128]{2,1,0:T(2,128)} copy(f32[128,2,128]{2,0,1:T(8,128)} %bitcast.4) | data formatting | bytes 262144 | tf_op jit(solution)/shard_map/transpose | solution.py:488

commit v4 on v3

--- a/solution.py
+++ b/solution.py
@@ -55,11 +55,11 @@
 
 def kernel(
     Y, Z, X,
-    spec_hbm, mask_hbm, pair_hbm, owner_hbm, table_hbm, out_ref,
+    spec_hbm, mask_hbm, pair_hbm, owner_hbm, table_hbm, own_hbm, r2_in,
     spec_ref, mask_ref, pair_ref, owner_ref, table, perm_a, perm_b, perm_l, perm_s,
-    pka, pkb, p1a, p1b, every_a, every_b, lists, acc, r1_out, r1_in, r2_out, r2_in,
+    pka, pkb, p1a, p1b, every_a, every_b, lists, acc, r1_out, r1_in, r2_out, own, ids,
     in_sem, tab_sem, p1a_s, p1a_r, p1b_s, p1b_r, ring_s, ring_r, l2_s, l2_r, l3_s, l3_r,
-    r1_s, r1_r, r2_s, r2_r,
+    r1_s, r1_r, r2_s, r2_r, own_s,
 ):
     D = 2 * Y * Z
     NST = 2 * D
@@ -308,17 +308,17 @@
     st_a = st_a.astype(F32)
     st_b = ka.astype(F32)
 
-    def slots_of(o):
+    def slots_of(which, o):
         match = owner_id == o.astype(F32)
         mf = match.astype(F32)
         before = dot(mf.astype(BF), tri)
         picks = [mf * (before == float(i)).astype(F32) for i in range(2)]
-        first = jnp.concatenate(
-            [jnp.sum(p * (first_id + 1.0), axis=1, keepdims=True) for p in picks], axis=0
-        ) - 1.0
-        second = jnp.concatenate(
-            [jnp.sum(p * (second_id + 1.0), axis=1, keepdims=True) for p in picks], axis=0
-        ) - 1.0
+        lane = iota((D, 128), 1)
+        for i, p in enumerate(picks):
+            first = jnp.sum(p * (first_id + 1.0), axis=1, keepdims=True)
+            second = jnp.sum(p * (second_id + 1.0), axis=1, keepdims=True)
+            ids[which, pl.ds(i, D, stride=2), :] = jnp.where(lane == 0, first, second) - 1.0
+        first, second = ids[which, :, 0:1], ids[which, :, 1:2]
         one_b = [onehot(st_b == first), onehot(st_b == second)]
         one_a = [onehot(st_a == first), onehot(st_a == second)]
         both = dot(one_b[0], mask_st) * dot(one_b[1], mask_st)
@@ -326,7 +326,7 @@
         here = jnp.where(iota(both.shape, 1) == x, both, 0.0)
         return (one_a, one_b), jnp.sum(here, axis=1, keepdims=True) / count
 
-    slots = [slots_of(me - c + sib), slots_of(me)]
+    slots = [slots_of(0, me - c + sib), slots_of(1, me)]
     for copy in tab_copies:
         copy.wait()
 
@@ -394,10 +394,11 @@
 
     def r2_copy(i):
         return pltpu.make_async_remote_copy(
-            src_ref=r2_out.at[i], dst_ref=r2_in.at[i], send_sem=r2_s.at[i],
+            src_ref=r2_out.at[i], dst_ref=r2_in.at[i - 1], send_sem=r2_s.at[i],
             recv_sem=r2_r.at[i], device_id=(me, (x + i) % X), device_id_type=MESH,
         )
 
+    own_copy = pltpu.make_async_copy(own, own_hbm, own_s)
     parts = stack_of(0, w)
     for side in range(NS):
         r1_out[side] = finish(0, side, parts)
@@ -413,12 +414,8 @@
                 r2_out[i] = piece.astype(BF)
                 r2_copy(i).start()
             else:
-                result = piece
-    for i in range(1, X):
-        r2_copy(i).wait_recv()
-        result = result + r2_in[i].astype(F32)
-    out_ref[...] = result.reshape(2, D, 128)
-
+                own[...] = piece
+                own_copy.start()
     wait_bytes(p1a.at[pl.ds(0, GA - 1)], p1a_s)
     wait_bytes(p1b.at[pl.ds(0, GB - 1)], p1b_s)
     if Z > 1:
@@ -434,6 +431,9 @@
         r1_copy(side).wait_send()
     for i in range(1, X):
         r2_copy(i).wait_send()
+    own_copy.wait()
+    for i in range(1, X):
+        r2_copy(i).wait_recv()
 
 
 def body(dims, spectra, masks, pairs, owners):
@@ -448,11 +448,14 @@
     sides = 2 if X > 1 else 1
     wide = lags // sides
     dma = pltpu.SemaphoreType.DMA
-    stacks = pl.pallas_call(
+    own, others = pl.pallas_call(
         functools.partial(kernel, Y, Z, X),
-        out_shape=jax.ShapeDtypeStruct((2, D, 128), F32),
+        out_shape=(
+            jax.ShapeDtypeStruct((2 * D, 128), F32),
+            jax.ShapeDtypeStruct((max(X - 1, 1), 2 * D, 128), BF),
+        ),
         in_specs=[pl.BlockSpec(memory_space=pl.ANY)] * 5,
-        out_specs=pl.BlockSpec(memory_space=pltpu.VMEM),
+        out_specs=[pl.BlockSpec(memory_space=pl.ANY)] * 2,
         scratch_shapes=[
             pltpu.VMEM(spectra.shape, BF),
             pltpu.VMEM(masks.shape, I32),
@@ -474,18 +477,21 @@
             pltpu.VMEM((sides, 2 * D, wide), F32),
             pltpu.VMEM((sides, 2 * D, wide), F32),
             pltpu.VMEM((X, 2 * D, 128), BF),
-            pltpu.VMEM((X, 2 * D, 128), BF),
+            pltpu.VMEM((2 * D, 128), F32),
+            pltpu.VMEM((2, 2 * D, 128), F32),
             dma((4,)), dma((X,)), dma, dma, dma, dma,
             dma((2, W, 2, max(Y, Z) // 2)),
             dma((2, W, 2, max(Y, Z) // 2)),
             dma, dma, dma, dma,
-            dma((sides,)), dma((sides,)), dma((X,)), dma((X,)),
+            dma((sides,)), dma((sides,)), dma((X,)), dma((X,)), dma,
         ],
         compiler_params=pltpu.CompilerParams(
             collective_id=0, has_side_effects=True, vmem_limit_bytes=63 * 1024 * 1024
         ),
     )(spectra, masks, pairs.T, owners.T, table)
-    return stacks.transpose(1, 0, 2).reshape(2 * D, 128)
+    for i in range(X - 1):
+        own = own + others[i].astype(F32)
+    return own
 
 
 def dims_of(mesh):

time: 43.8 us -> 43.2 us (0.986)
  local copies, waits for them, and re-layouts: 1.66 us -> 0 us
  other arithmetic: 0 us -> 1.65 us
  Pallas kernels: 42 us -> 41.3 us
    transpose x1 -> x0, local copies, waits for them, and re-layouts: 1.66 us -> none  [body(): return stacks.transpose(1, 0, 2).reshape(2 * D, 128)]
    add x0 -> x1, other arithmetic: none -> 1.65 us  [body(): own = own + others[i].astype(F32)]
    pallas_call x1, Pallas kernels: 42 us -> 41.3 us  [body(): pl.pallas_call(functools.partial(kernel, Y, Z, X), out_shape=(jax.ShapeDt...]
where the time goes in v4:
time: 43.2 us; the launch traced here: 43 us
  Pallas kernels  41.3 us (96%)
  other arithmetic  1.65 us (4%)
    pallas_call x1, Pallas kernels, body(): pl.pallas_call(functools.partial(kernel, Y, Z, X), out_shape=(jax.ShapeDt...  41.3 us
    add x1, other arithmetic, body(): own = own + others[i].astype(F32)  1.65 us

profile of v4, /device:TPU:3, one launch (start us, length us, event | category | flops | bytes accessed | tf_op | source)
XLA Modules:
  0.0 43.0 jit_solution(7737008767306627902)
XLA Ops:
  0.0 41.3 %shard_map.55 = (f32[256,128]{1,0:T(8,128)}, bf16[3,256,128]{2,1,0:T(8,128)(2,1)}) custom-call(bf16[2,1,2,2048]{3,2,1,0:T(2,128)(2,1)} %spec_hbm.1, s32[2,4]{1,0:T(2,128)} %mask_hbm.1, s32[2,128]{1,0:T(2,128)} %bitcast.11, s32[1,128]{1,0:T(1,128)} %bitcast.12, bf16[2,4,2,2,2,512,128]{6,5,4,3,2,1,0:T(8,128)(2,1)} %constant.2.clone.table_hbm), custom_call_target="tpu_custom_call" | custom-call | tf_op jit(solution)/shard_map/pallas_call | solution.py:451
  41.4 1.7 %convert_add_fusion = f32[256,128]{1,0:T(8,128)} fusion(f32[256,128]{1,0:T(8,128)} %get-tuple-element.7, bf16[3,256,128]{2,1,0:T(8,128)(2,1)} %get-tuple-element.8), kind=kLoop, calls=%fused_computation | loop fusion | flops 196608 | bytes 458752 | tf_op jit(solution)/shard_map/add | solution.py:493

commit v5 on v4

--- a/solution.py
+++ b/solution.py
@@ -247,6 +247,12 @@
                     col = (ri * jw + j) * 128
                     every[w, pos, :, col : col + 128] = block[row : row + 2 * size]
 
+    n, k = iota((4 * D, 4 * D), 0), iota((4 * D, 4 * D), 1)
+    d, q = mod(n, D), div(n, D)
+    pos = div(d, 2 * Z) * 2 + mod(d, 2)
+    src = (div(pos, share) * Z + mod(div(d, 2), Z)) * (4 * share) + q * share + mod(pos, share)
+    perm_s[...] = onehot(k == src)
+
     wait_bytes(p1a.at[pl.ds(0, GA - 1)], p1a_r)
 
     def lists_x():
@@ -258,13 +264,6 @@
                 device_id=(me, (x + i) % X), device_id_type=MESH,
             ).start()
 
-    def prepare():
-        n, k = iota((4 * D, 4 * D), 0), iota((4 * D, 4 * D), 1)
-        d, q = mod(n, D), div(n, D)
-        pos = div(d, 2 * Z) * 2 + mod(d, 2)
-        src = (div(pos, share) * Z + mod(div(d, 2), Z)) * (4 * share) + q * share + mod(pos, share)
-        perm_s[...] = onehot(k == src)
-
     def lists_z():
         lists[x, z] = dot(perm_l[...], p1a[:, PR : PR + 16, :].reshape(GA * 16, 128)).astype(BF)
         for i in far_first(Z):
@@ -280,7 +279,6 @@
     wait_bytes(p1b.at[pl.ds(0, GB - 1)], p1b_r)
     place(every_b, y, perm_b, p1b[...].reshape(GB * PR, 128), GB)
     start_direct(1)
-    prepare()
     lists_x()
 
     forward(0, 0)
@@ -341,10 +339,11 @@
     def stack_of(which, w):
         parts = []
         for h, every in enumerate((every_a, every_b)):
-            ones = slots[which][0][h]
-            stations = every[w].reshape(NST, 2 * quarter)
-            f = dot(ones[0], stations)
-            s = dot(ones[1], stations)
+            firsts = [slots[g][0][h][0] for g in which]
+            seconds = [slots[g][0][h][1] for g in which]
+            both = dot(jnp.concatenate(firsts + seconds, axis=0), every[w].reshape(NST, 2 * quarter))
+            rows = both.shape[0] // 2
+            f, s = both[:rows], both[rows:]
             fr, fi = f[:, :quarter], f[:, quarter:]
             sr, si = s[:, :quarter], s[:, quarter:]
             stack = jnp.concatenate([fr * sr + fi * si, fi * sr - fr * si], axis=1)
@@ -369,13 +368,14 @@
     for w in range(W - 1):
         drain(0, w)
         drain(1, w)
-        for which in range(2):
-            parts = stack_of(which, w)
-            for side in range(NS):
-                value = product(parts, w, side)
+        parts = stack_of((0, 1), w)
+        for side in range(NS):
+            value = product(parts, w, side)
+            for which in range(2):
+                piece = value[which * 2 * D : (which + 1) * 2 * D]
                 if w > 0:
-                    value = value + acc[which, side]
-                acc[which, side] = value
+                    piece = piece + acc[which, side]
+                acc[which, side] = piece
     w = W - 1
     drain(0, w)
     drain(1, w)
@@ -399,14 +399,13 @@
         )
 
     own_copy = pltpu.make_async_copy(own, own_hbm, own_s)
-    parts = stack_of(0, w)
+    parts = stack_of((0,), w)
     for side in range(NS):
         r1_out[side] = finish(0, side, parts)
         r1_copy(side).start()
-    parts = stack_of(1, w)
+    parts = stack_of((1,), w)
     for side in range(NS):
         acc[1, side] = finish(1, side, parts)
-    for side in range(NS):
         r1_copy(side).wait_recv()
         for m, i in enumerate(sides[side]):
             piece = acc[1, side, :, m * 128 : (m + 1) * 128] + r1_in[side, :, m * 128 : (m + 1) * 128]

time: 43.2 us -> 43 us (level)
  the two profiles are of different devices: /device:TPU:3 before, /device:TPU:2 now
where the time goes in v5:
time: 43 us; the launch traced here: 42.8 us
  Pallas kernels  41.1 us (96%)
  other arithmetic  1.65 us (4%)
    pallas_call x1, Pallas kernels, body(): pl.pallas_call(functools.partial(kernel, Y, Z, X), out_shape=(jax.ShapeDt...  41.1 us
    add x1, other arithmetic, body(): own = own + others[i].astype(F32)  1.65 us

profile of v5, /device:TPU:2, one launch (start us, length us, event | category | flops | bytes accessed | tf_op | source)
XLA Modules:
  0.0 42.8 jit_solution(3893112655287325217)
XLA Ops:
  0.0 41.1 %shard_map.55 = (f32[256,128]{1,0:T(8,128)}, bf16[3,256,128]{2,1,0:T(8,128)(2,1)}) custom-call(bf16[2,1,2,2048]{3,2,1,0:T(2,128)(2,1)} %spec_hbm.1, s32[2,4]{1,0:T(2,128)} %mask_hbm.1, s32[2,128]{1,0:T(2,128)} %bitcast.11, s32[1,128]{1,0:T(1,128)} %bitcast.12, bf16[2,4,2,2,2,512,128]{6,5,4,3,2,1,0:T(8,128)(2,1)} %constant.2.clone.table_hbm), custom_call_target="tpu_custom_call" | custom-call | tf_op jit(solution)/shard_map/pallas_call | solution.py:450
  41.1 1.7 %convert_add_fusion = f32[256,128]{1,0:T(8,128)} fusion(f32[256,128]{1,0:T(8,128)} %get-tuple-element.7, bf16[3,256,128]{2,1,0:T(8,128)(2,1)} %get-tuple-element.8), kind=kLoop, calls=%fused_computation | loop fusion | flops 196608 | bytes 458752 | tf_op jit(solution)/shard_map/add | solution.py:492
